TPU v7x, 32 devices: a whole 2x2x4 slice. The times are simulated.
32 devices in a mesh: groups: 2 (over x), seg: 8 (over z, y), space: 2 (over core).
Axes of the slice: x: 2, y: 2, z: 4, core: 2. Of those that a mesh axis runs over, the one named last changes fastest.
Arguments:
- trajectory: float32 [16, 32, 2, 16, 256], P(('groups', 'seg'), None, None, 'space'), parts along dimension 0, may hold values from -3 to 3
Outputs:
- corrected: float32 [16, 32, 2, 16, 256], P(('groups', 'seg'), None, None, 'space'), parts along dimension 0
There are 2 independent parts, one for each index of `groups`. A program takes and returns all parts, laid end to end along the dimension named above; each array names one. Nothing has to cross between parts.
All inputs are finite; a program needn't handle non-finite values.
Results may differ from a plain program's by a relative error of at most 0.0003.
Values sent between devices are 32-bit elements; how exact they have to be, the bound alone decides.
A program may use at most 64 MiB of HBM per device.

v0:
```python
import jax
import jax.numpy as jnp
import numpy as np
from jax import lax
from jax.sharding import PartitionSpec as P

SWEEPS = 3
CSTEPS = 4
COARSEN = 4


SEGMENT_TIME = 0.5
VISCOSITY = 0.05


def with_halo(cells, sides, width):
    for axis, dim in sides:
        count = lax.axis_size(axis)
        head = lax.slice_in_dim(cells, 0, width, axis=dim)
        tail = lax.slice_in_dim(cells, cells.shape[dim] - width, cells.shape[dim], axis=dim)
        cells = jnp.concatenate(
            [
                lax.ppermute(tail, axis, [(i, (i + 1) % count) for i in range(count)]),
                cells,
                lax.ppermute(head, axis, [((i + 1) % count, i) for i in range(count)]),
            ],
            axis=dim,
        )
    return cells


def passed_along(value, axis, steps):
    count = lax.axis_size(axis)
    initial, last = (max(0, -steps), min(count, count - steps))
    return lax.ppermute(value, axis, [(source, source + steps) for source in range(initial, last)])


def integration_table(count, length):
    last = count - 1
    orders = np.arange(count)
    angles = np.pi * (last - orders) / last
    points = np.cos(angles)
    cheb = np.cos(np.outer(angles, orders))
    weights = np.where((orders == 0) | (orders == last), 0.5, 1.0)
    inverse = 2.0 / last * weights[:, None] * cheb.T * weights[None, :]
    upper = orders + 1.0
    lower = np.maximum(orders - 1.0, 1.0)
    general = np.cos(np.outer(angles, upper)) / (2.0 * upper) - np.cos(
        np.outer(angles, orders - 1.0)
    ) / (2.0 * lower)
    general = general - (
        (-1.0) ** (orders + 1) / (2.0 * upper) - (-1.0) ** np.abs(orders - 1) / (2.0 * lower)
    )
    integral = np.where(
        orders[None, :] == 0,
        points[:, None] + 1.0,
        np.where(orders[None, :] == 1, (points[:, None] ** 2 - 1.0) / 2.0, general),
    )
    return (integral @ inverse * (length / 2.0)).astype(np.float32)


def strip_rows(field):
    return with_halo(field, (("space", 1),), 1)


def burgers_rhs(padded, spacing):
    center = padded[..., 1:-1, :]
    north = padded[..., 2:, :]
    south = padded[..., :-2, :]
    east = jnp.roll(center, -1, axis=-1)
    west = jnp.roll(center, 1, axis=-1)
    grad_x = (north - south) / (2.0 * spacing)
    grad_y = (east - west) / (2.0 * spacing)
    lapl = (north + south + east + west - 4.0 * center) / (spacing * spacing)
    vel_u = center[..., 0:1, :, :]
    vel_v = center[..., 1:2, :, :]
    return VISCOSITY * lapl - (vel_u * grad_x + vel_v * grad_y)


def picard_sweep(padded, int_table):
    slope = burgers_rhs(padded, 1.0)
    begin = padded[0:1, :, 1:-1, :]
    flat_slope = slope.reshape(slope.shape[0], -1)
    integral = jnp.dot(int_table, flat_slope, precision=lax.Precision.HIGHEST)
    return begin + integral.reshape(slope.shape)


def restrict(field):
    shaped = field.reshape(
        field.shape[:-2]
        + (field.shape[-2] // COARSEN, COARSEN, field.shape[-1] // COARSEN, COARSEN)
    )
    return jnp.mean(shaped, axis=(-3, -1))


def prolong(field):
    return jnp.repeat(jnp.repeat(field, COARSEN, axis=-2), COARSEN, axis=-1)


def coarse_prop(coarse_now, pad_rows):
    step_len = SEGMENT_TIME / CSTEPS
    for number in range(CSTEPS):
        coarse_now = coarse_now + step_len * burgers_rhs(pad_rows(coarse_now), float(COARSEN))
    return coarse_now


def per_device(trajectory):
    node_count = trajectory.shape[1]
    int_table = jnp.asarray(integration_table(node_count, SEGMENT_TIME))
    previous = trajectory[0]
    current = previous
    for number in range(SWEEPS):
        padded = with_halo(current, (("space", 2),), 1)
        current = picard_sweep(padded, int_table)
    fine_end = current[-1]
    old_start = previous[0]
    seg_index = lax.axis_index("seg")
    prev_end = passed_along(fine_end, "seg", 1)
    r_end = restrict(fine_end)
    r_start = restrict(old_start)
    r_end_x, r_start_x = (r_end, r_start)
    jump_own = r_end_x - coarse_prop(r_start_x, strip_rows)
    seg_count = lax.axis_size("seg")

    def advance(turn, carry):
        stepped = coarse_prop(carry, strip_rows) + jump_own
        moved = passed_along(stepped, "seg", 1)
        return jnp.where(seg_index == turn + 1, moved, carry)

    coarse_here = lax.fori_loop(0, seg_count - 1, advance, r_start_x)
    fixed = prev_end + prolong(coarse_here - restrict(prev_end)) - old_start
    shift_here = jnp.where(seg_index > 0, fixed, jnp.zeros_like(fixed))
    return (current + shift_here[None])[None]


def solution(mesh):
    placed = (P(("groups", "seg"), None, None, "space", None),)
    return jax.shard_map(
        per_device,
        mesh=mesh,
        in_specs=placed,
        out_specs=P(("groups", "seg"), None, None, "space", None),
        check_vma=False,
    )
```

profile of v0, /device:TPU:27, one launch (start us, length us, event | category | flops | bytes accessed | tf_op | source)
XLA Modules:
  0.0 120.8 jit_solution(2109952160042113576)
XLA Ops:
  0.0 1.4 %fusion.40 = (f32[32,2,1,256]{3,2,1,0:T(1,128)S(1)}, f32[32,2,1,256]{3,2,1,0:T(1,128)S(1)}) fusion(f32[32,2,8,256]{3,2,1,0:T(8,128)} %bitcast.97), kind=kLoop, calls=%fused_computation.128 | loop fusion | bytes 262144 | tf_op jit(solution)/shard_map/slice | solution.py:20
  1.4 0.7 collective-permute-start.9
  2.2 0.7 fusion.33
  6.0 0.6 collective-permute-done.18
  7.6 0.6 collective-permute-done.20
  12.4 0.7 collective-permute-done.11
  19.0 3.2 %collective-permute-start.15 = (f32[2,8,256]{1,2,0:T(8,128)S(1)}, f32[2,8,256]{1,2,0:T(8,128)S(1)}, u32[]{:S(2)}, u32[]{:S(2)}) collective-permute-start(f32[2,8,256]{1,2,0:T(8,128)S(1)} %bitcast.115), channel_id=1, source_target_pairs={{0,2},{2,4},{4,6},{6,8},{8,10},{10,12},{12,14},{1,3},{3,5},{5,7},{... | collective-permute-start | bytes 49160 | tf_op jit(solution)/shard_map/ppermute | solution.py:35
  22.9 6.6 %collective-permute-done.15 = f32[2,8,256]{1,2,0:T(8,128)S(1)} collective-permute-done((f32[2,8,256]{1,2,0:T(8,128)S(1)}, f32[2,8,256]{1,2,0:T(8,128)S(1)}, u32[]{:S(2)}, u32[]{:S(2)}) %collective-permute-start.15) | collective-permute-done | bytes 16416 | tf_op jit(solution)/shard_map/ppermute | solution.py:35
  30.3 89.4 %while.16 = (s32[]{:T(128)}, f32[2,2,64]{2,1,0:T(2,128)S(1)}, s32[]{:T(128)}, f32[2,2,64]{2,1,0:T(2,128)S(1)}, s32[]{:T(128)}) while((s32[]{:T(128)}, f32[2,2,64]{2,1,0:T(2,128)S(1)}, s32[]{:T(128)}, f32[2,2,64]{2,1,0:T(2,128)S(1)}, s32[]{:T(128)}) %tuple.116), condition=%wide.region_3.4_spmd, body=%wide.region_2.3_spmd.sunk | while | flops 19971 | bytes 82351 | solution.py:130
  30.3 1.1 collective-permute-start
  33.2 0.6 collective-permute-done.2
  34.8 0.6 collective-permute-done.4
  36.5 0.6 collective-permute-done.6
  37.4 2.2 %collective-permute-start.8 = (f32[2,2,64]{2,1,0:T(2,128)S(1)}, f32[2,2,64]{2,1,0:T(2,128)S(1)}, u32[]{:S(2)}, u32[]{:S(2)}) collective-permute-start(f32[2,2,64]{2,1,0:T(2,128)S(1)} %add_add_fusion.3), channel_id=1, source_target_pairs={{0,2},{2,4},{4,6},{6,8},{8,10},{10,12},{12,14},{1,3},{3,5},{5,7},{... | collective-permute-start | bytes 3080 | tf_op jit(solution)/shard_map/while/body/eval_jaxpr/ppermute | solution.py:35
  39.7 3.0 %collective-permute-done.8 = f32[2,2,64]{2,1,0:T(2,128)S(1)} collective-permute-done((f32[2,2,64]{2,1,0:T(2,128)S(1)}, f32[2,2,64]{2,1,0:T(2,128)S(1)}, u32[]{:S(2)}, u32[]{:S(2)}) %collective-permute-start.8) | collective-permute-done | bytes 1056 | tf_op jit(solution)/shard_map/while/body/eval_jaxpr/ppermute | solution.py:35
  42.7 1.5 %collective-permute-start = (f32[2,1,64]{2,1,0:T(1,128)S(1)}, f32[2,1,64]{2,1,0:T(1,128)S(1)}, u32[]{:S(2)}, u32[]{:S(2)}) collective-permute-start(f32[2,1,64]{2,1,0:T(1,128)S(1)} %get-tuple-element.291), channel_id=1, source_target_pairs={{1,0},{0,1},{3,2},{2,3},{5,4},{4,5},{7,6},{6,7},{9,8},{8,9},{11,10... | collective-permute-start | bytes 1544 | tf_op jit(solution)/shard_map/while/body/eval_jaxpr/ppermute | solution.py:25
  46.1 0.6 collective-permute-done.2
  47.7 0.6 collective-permute-done.4
  49.4 0.6 collective-permute-done.6
  50.3 1.9 %collective-permute-start.8 = (f32[2,2,64]{2,1,0:T(2,128)S(1)}, f32[2,2,64]{2,1,0:T(2,128)S(1)}, u32[]{:S(2)}, u32[]{:S(2)}) collective-permute-start(f32[2,2,64]{2,1,0:T(2,128)S(1)} %add_add_fusion.3), channel_id=1, source_target_pairs={{0,2},{2,4},{4,6},{6,8},{8,10},{10,12},{12,14},{1,3},{3,5},{5,7},{... | collective-permute-start | bytes 3080 | tf_op jit(solution)/shard_map/while/body/eval_jaxpr/ppermute | solution.py:35
  52.2 3.3 %collective-permute-done.8 = f32[2,2,64]{2,1,0:T(2,128)S(1)} collective-permute-done((f32[2,2,64]{2,1,0:T(2,128)S(1)}, f32[2,2,64]{2,1,0:T(2,128)S(1)}, u32[]{:S(2)}, u32[]{:S(2)}) %collective-permute-start.8) | collective-permute-done | bytes 1056 | tf_op jit(solution)/shard_map/while/body/eval_jaxpr/ppermute | solution.py:35
  55.5 1.5 %collective-permute-start = (f32[2,1,64]{2,1,0:T(1,128)S(1)}, f32[2,1,64]{2,1,0:T(1,128)S(1)}, u32[]{:S(2)}, u32[]{:S(2)}) collective-permute-start(f32[2,1,64]{2,1,0:T(1,128)S(1)} %get-tuple-element.291), channel_id=1, source_target_pairs={{1,0},{0,1},{3,2},{2,3},{5,4},{4,5},{7,6},{6,7},{9,8},{8,9},{11,10... | collective-permute-start | bytes 1544 | tf_op jit(solution)/shard_map/while/body/eval_jaxpr/ppermute | solution.py:25
  58.9 0.6 collective-permute-done.2
  60.5 0.6 collective-permute-done.4
  62.2 0.6 collective-permute-done.6
  63.1 1.9 %collective-permute-start.8 = (f32[2,2,64]{2,1,0:T(2,128)S(1)}, f32[2,2,64]{2,1,0:T(2,128)S(1)}, u32[]{:S(2)}, u32[]{:S(2)}) collective-permute-start(f32[2,2,64]{2,1,0:T(2,128)S(1)} %add_add_fusion.3), channel_id=1, source_target_pairs={{0,2},{2,4},{4,6},{6,8},{8,10},{10,12},{12,14},{1,3},{3,5},{5,7},{... | collective-permute-start | bytes 3080 | tf_op jit(solution)/shard_map/while/body/eval_jaxpr/ppermute | solution.py:35
  65.0 3.3 %collective-permute-done.8 = f32[2,2,64]{2,1,0:T(2,128)S(1)} collective-permute-done((f32[2,2,64]{2,1,0:T(2,128)S(1)}, f32[2,2,64]{2,1,0:T(2,128)S(1)}, u32[]{:S(2)}, u32[]{:S(2)}) %collective-permute-start.8) | collective-permute-done | bytes 1056 | tf_op jit(solution)/shard_map/while/body/eval_jaxpr/ppermute | solution.py:35
  68.3 1.5 %collective-permute-start = (f32[2,1,64]{2,1,0:T(1,128)S(1)}, f32[2,1,64]{2,1,0:T(1,128)S(1)}, u32[]{:S(2)}, u32[]{:S(2)}) collective-permute-start(f32[2,1,64]{2,1,0:T(1,128)S(1)} %get-tuple-element.291), channel_id=1, source_target_pairs={{1,0},{0,1},{3,2},{2,3},{5,4},{4,5},{7,6},{6,7},{9,8},{8,9},{11,10... | collective-permute-start | bytes 1544 | tf_op jit(solution)/shard_map/while/body/eval_jaxpr/ppermute | solution.py:25
  71.7 0.6 collective-permute-done.2
  73.3 0.6 collective-permute-done.4
  75.0 0.6 collective-permute-done.6
  75.9 1.9 %collective-permute-start.8 = (f32[2,2,64]{2,1,0:T(2,128)S(1)}, f32[2,2,64]{2,1,0:T(2,128)S(1)}, u32[]{:S(2)}, u32[]{:S(2)}) collective-permute-start(f32[2,2,64]{2,1,0:T(2,128)S(1)} %add_add_fusion.3), channel_id=1, source_target_pairs={{0,2},{2,4},{4,6},{6,8},{8,10},{10,12},{12,14},{1,3},{3,5},{5,7},{... | collective-permute-start | bytes 3080 | tf_op jit(solution)/shard_map/while/body/eval_jaxpr/ppermute | solution.py:35
  77.8 3.3 %collective-permute-done.8 = f32[2,2,64]{2,1,0:T(2,128)S(1)} collective-permute-done((f32[2,2,64]{2,1,0:T(2,128)S(1)}, f32[2,2,64]{2,1,0:T(2,128)S(1)}, u32[]{:S(2)}, u32[]{:S(2)}) %collective-permute-start.8) | collective-permute-done | bytes 1056 | tf_op jit(solution)/shard_map/while/body/eval_jaxpr/ppermute | solution.py:35
  81.2 1.5 %collective-permute-start = (f32[2,1,64]{2,1,0:T(1,128)S(1)}, f32[2,1,64]{2,1,0:T(1,128)S(1)}, u32[]{:S(2)}, u32[]{:S(2)}) collective-permute-start(f32[2,1,64]{2,1,0:T(1,128)S(1)} %get-tuple-element.291), channel_id=1, source_target_pairs={{1,0},{0,1},{3,2},{2,3},{5,4},{4,5},{7,6},{6,7},{9,8},{8,9},{11,10... | collective-permute-start | bytes 1544 | tf_op jit(solution)/shard_map/while/body/eval_jaxpr/ppermute | solution.py:25
  86.2 0.6 collective-permute-done.4
  88.8 1.9 %collective-permute-start.8 = (f32[2,2,64]{2,1,0:T(2,128)S(1)}, f32[2,2,64]{2,1,0:T(2,128)S(1)}, u32[]{:S(2)}, u32[]{:S(2)}) collective-permute-start(f32[2,2,64]{2,1,0:T(2,128)S(1)} %add_add_fusion.3), channel_id=1, source_target_pairs={{0,2},{2,4},{4,6},{6,8},{8,10},{10,12},{12,14},{1,3},{3,5},{5,7},{... | collective-permute-start | bytes 3080 | tf_op jit(solution)/shard_map/while/body/eval_jaxpr/ppermute | solution.py:35
  90.7 3.3 %collective-permute-done.8 = f32[2,2,64]{2,1,0:T(2,128)S(1)} collective-permute-done((f32[2,2,64]{2,1,0:T(2,128)S(1)}, f32[2,2,64]{2,1,0:T(2,128)S(1)}, u32[]{:S(2)}, u32[]{:S(2)}) %collective-permute-start.8) | collective-permute-done | bytes 1056 | tf_op jit(solution)/shard_map/while/body/eval_jaxpr/ppermute | solution.py:35
  94.0 1.5 %collective-permute-start = (f32[2,1,64]{2,1,0:T(1,128)S(1)}, f32[2,1,64]{2,1,0:T(1,128)S(1)}, u32[]{:S(2)}, u32[]{:S(2)}) collective-permute-start(f32[2,1,64]{2,1,0:T(1,128)S(1)} %get-tuple-element.291), channel_id=1, source_target_pairs={{1,0},{0,1},{3,2},{2,3},{5,4},{4,5},{7,6},{6,7},{9,8},{8,9},{11,10... | collective-permute-start | bytes 1544 | tf_op jit(solution)/shard_map/while/body/eval_jaxpr/ppermute | solution.py:25
  97.4 0.6 collective-permute-done.2
  99.0 0.6 collective-permute-done.4
  101.6 1.9 %collective-permute-start.8 = (f32[2,2,64]{2,1,0:T(2,128)S(1)}, f32[2,2,64]{2,1,0:T(2,128)S(1)}, u32[]{:S(2)}, u32[]{:S(2)}) collective-permute-start(f32[2,2,64]{2,1,0:T(2,128)S(1)} %add_add_fusion.3), channel_id=1, source_target_pairs={{0,2},{2,4},{4,6},{6,8},{8,10},{10,12},{12,14},{1,3},{3,5},{5,7},{... | collective-permute-start | bytes 3080 | tf_op jit(solution)/shard_map/while/body/eval_jaxpr/ppermute | solution.py:35
  103.5 3.3 %collective-permute-done.8 = f32[2,2,64]{2,1,0:T(2,128)S(1)} collective-permute-done((f32[2,2,64]{2,1,0:T(2,128)S(1)}, f32[2,2,64]{2,1,0:T(2,128)S(1)}, u32[]{:S(2)}, u32[]{:S(2)}) %collective-permute-start.8) | collective-permute-done | bytes 1056 | tf_op jit(solution)/shard_map/while/body/eval_jaxpr/ppermute | solution.py:35
  106.8 1.5 %collective-permute-start = (f32[2,1,64]{2,1,0:T(1,128)S(1)}, f32[2,1,64]{2,1,0:T(1,128)S(1)}, u32[]{:S(2)}, u32[]{:S(2)}) collective-permute-start(f32[2,1,64]{2,1,0:T(1,128)S(1)} %get-tuple-element.291), channel_id=1, source_target_pairs={{1,0},{0,1},{3,2},{2,3},{5,4},{4,5},{7,6},{6,7},{9,8},{8,9},{11,10... | collective-permute-start | bytes 1544 | tf_op jit(solution)/shard_map/while/body/eval_jaxpr/ppermute | solution.py:25
  110.2 0.6 collective-permute-done.2
  111.8 0.6 collective-permute-done.4
  114.4 1.9 %collective-permute-start.8 = (f32[2,2,64]{2,1,0:T(2,128)S(1)}, f32[2,2,64]{2,1,0:T(2,128)S(1)}, u32[]{:S(2)}, u32[]{:S(2)}) collective-permute-start(f32[2,2,64]{2,1,0:T(2,128)S(1)} %add_add_fusion.3), channel_id=1, source_target_pairs={{0,2},{2,4},{4,6},{6,8},{8,10},{10,12},{12,14},{1,3},{3,5},{5,7},{... | collective-permute-start | bytes 3080 | tf_op jit(solution)/shard_map/while/body/eval_jaxpr/ppermute | solution.py:35
  116.3 3.3 %collective-permute-done.8 = f32[2,2,64]{2,1,0:T(2,128)S(1)} collective-permute-done((f32[2,2,64]{2,1,0:T(2,128)S(1)}, f32[2,2,64]{2,1,0:T(2,128)S(1)}, u32[]{:S(2)}, u32[]{:S(2)}) %collective-permute-start.8) | collective-permute-done | bytes 1056 | tf_op jit(solution)/shard_map/while/body/eval_jaxpr/ppermute | solution.py:35
  120.0 0.9 add_add_fusion.1
  (330 shorter events, 47.5 us)
Async XLA Ops:
  1.4 7.9 %collective-permute-start.9 = (f32[32,2,1,256]{3,2,1,0:T(1,128)S(1)}, f32[32,2,1,256]{3,2,1,0:T(1,128)S(1)}, u32[]{:S(2)}, u32[]{:S(2)}) collective-permute-start(f32[32,2,1,256]{3,2,1,0:T(1,128)S(1)} %get-tuple-element.193), channel_id=1, source_target_pairs={{1,0},{0,1},{3,2},{2,3},{5,4},{4,5},{7,6},{6,7},{9,8},{8,9},{11,10... | collective-permute-start | bytes 196616 | tf_op jit(solution)/shard_map/ppermute | solution.py:25
  2.1 7.2 %collective-permute-start.10 = (f32[32,2,1,256]{3,2,1,0:T(1,128)S(1)}, f32[32,2,1,256]{3,2,1,0:T(1,128)S(1)}, u32[]{:S(2)}, u32[]{:S(2)}) collective-permute-start(f32[32,2,1,256]{3,2,1,0:T(1,128)S(1)} %get-tuple-element.192), channel_id=1, source_target_pairs={{0,1},{1,0},{2,3},{3,2},{4,5},{5,4},{6,7},{7,6},{8,9},{9,8},{10,11... | collective-permute-start | bytes 196616 | tf_op jit(solution)/shard_map/ppermute | solution.py:23
  3.6 1.3 %collective-permute-start.16 = (f32[2,1,64]{2,1,0:T(1,128)S(1)}, f32[2,1,64]{2,1,0:T(1,128)S(1)}, u32[]{:S(2)}, u32[]{:S(2)}) collective-permute-start(f32[2,1,64]{2,1,0:T(1,128)S(1)} %get-tuple-element.225), channel_id=1, source_target_pairs={{1,0},{0,1},{3,2},{2,3},{5,4},{4,5},{7,6},{6,7},{9,8},{8,9},{11,10... | collective-permute-start | bytes 1544 | tf_op jit(solution)/shard_map/ppermute | solution.py:25
  5.5 1.1 collective-permute-start.18
  5.7 1.1 collective-permute-start.19
  7.1 1.1 collective-permute-start.20
  8.8 14.0 %collective-permute-start.22 = (f32[2,1,64]{2,1,0:T(1,128)S(1)}, f32[2,1,64]{2,1,0:T(1,128)S(1)}, u32[]{:S(2)}, u32[]{:S(2)}) collective-permute-start(f32[2,1,64]{2,1,0:T(1,128)S(1)} %get-tuple-element.201), channel_id=1, source_target_pairs={{1,0},{0,1},{3,2},{2,3},{5,4},{4,5},{7,6},{6,7},{9,8},{8,9},{11,10... | collective-permute-start | bytes 1544 | tf_op jit(solution)/shard_map/ppermute | solution.py:25
  9.0 13.8 %collective-permute-start.23 = (f32[2,1,64]{2,1,0:T(1,128)S(1)}, f32[2,1,64]{2,1,0:T(1,128)S(1)}, u32[]{:S(2)}, u32[]{:S(2)}) collective-permute-start(f32[2,1,64]{2,1,0:T(1,128)S(1)} %get-tuple-element.200), channel_id=1, source_target_pairs={{0,1},{1,0},{2,3},{3,2},{4,5},{5,4},{6,7},{7,6},{8,9},{9,8},{10,11... | collective-permute-start | bytes 1544 | tf_op jit(solution)/shard_map/ppermute | solution.py:23
  11.8 1.3 %collective-permute-start.11 = (f32[32,2,1,256]{3,2,1,0:T(1,128)S(1)}, f32[32,2,1,256]{3,2,1,0:T(1,128)S(1)}, u32[]{:S(2)}, u32[]{:S(2)}) collective-permute-start(f32[32,2,1,256]{3,2,1,0:T(1,128)S(1)} %get-tuple-element.185), channel_id=1, source_target_pairs={{1,0},{0,1},{3,2},{2,3},{5,4},{4,5},{7,6},{6,7},{9,8},{8,9},{11,10... | collective-permute-start | bytes 196616 | tf_op jit(solution)/shard_map/ppermute | solution.py:25
  12.1 1.3 %collective-permute-start.12 = (f32[32,2,1,256]{3,2,1,0:T(1,128)S(1)}, f32[32,2,1,256]{3,2,1,0:T(1,128)S(1)}, u32[]{:S(2)}, u32[]{:S(2)}) collective-permute-start(f32[32,2,1,256]{3,2,1,0:T(1,128)S(1)} %get-tuple-element.184), channel_id=1, source_target_pairs={{0,1},{1,0},{2,3},{3,2},{4,5},{5,4},{6,7},{7,6},{8,9},{9,8},{10,11... | collective-permute-start | bytes 196616 | tf_op jit(solution)/shard_map/ppermute | solution.py:23
  15.5 1.3 %collective-permute-start.13 = (f32[32,2,1,256]{3,2,1,0:T(1,128)S(1)}, f32[32,2,1,256]{3,2,1,0:T(1,128)S(1)}, u32[]{:S(2)}, u32[]{:S(2)}) collective-permute-start(f32[32,2,1,256]{3,2,1,0:T(1,128)S(1)} %get-tuple-element.177), channel_id=1, source_target_pairs={{1,0},{0,1},{3,2},{2,3},{5,4},{4,5},{7,6},{6,7},{9,8},{8,9},{11,10... | collective-permute-start | bytes 196616 | tf_op jit(solution)/shard_map/ppermute | solution.py:25
  15.9 1.3 %collective-permute-start.14 = (f32[32,2,1,256]{3,2,1,0:T(1,128)S(1)}, f32[32,2,1,256]{3,2,1,0:T(1,128)S(1)}, u32[]{:S(2)}, u32[]{:S(2)}) collective-permute-start(f32[32,2,1,256]{3,2,1,0:T(1,128)S(1)} %get-tuple-element.176), channel_id=1, source_target_pairs={{0,1},{1,0},{2,3},{3,2},{4,5},{5,4},{6,7},{7,6},{8,9},{9,8},{10,11... | collective-permute-start | bytes 196616 | tf_op jit(solution)/shard_map/ppermute | solution.py:23
  19.0 10.5 %collective-permute-start.15 = (f32[2,8,256]{1,2,0:T(8,128)S(1)}, f32[2,8,256]{1,2,0:T(8,128)S(1)}, u32[]{:S(2)}, u32[]{:S(2)}) collective-permute-start(f32[2,8,256]{1,2,0:T(8,128)S(1)} %bitcast.115), channel_id=1, source_target_pairs={{0,2},{2,4},{4,6},{6,8},{8,10},{10,12},{12,14},{1,3},{3,5},{5,7},{... | collective-permute-start | bytes 49160 | tf_op jit(solution)/shard_map/ppermute | solution.py:35
  30.3 1.9 %collective-permute-start = (f32[2,1,64]{2,1,0:T(1,128)S(1)}, f32[2,1,64]{2,1,0:T(1,128)S(1)}, u32[]{:S(2)}, u32[]{:S(2)}) collective-permute-start(f32[2,1,64]{2,1,0:T(1,128)S(1)} %get-tuple-element.291), channel_id=1, source_target_pairs={{1,0},{0,1},{3,2},{2,3},{5,4},{4,5},{7,6},{6,7},{9,8},{8,9},{11,10... | collective-permute-start | bytes 1544 | tf_op jit(solution)/shard_map/while/body/eval_jaxpr/ppermute | solution.py:25
  32.7 1.1 collective-permute-start.2
  34.3 1.1 collective-permute-start.4
  36.0 1.1 collective-permute-start.6
  37.4 5.2 %collective-permute-start.8 = (f32[2,2,64]{2,1,0:T(2,128)S(1)}, f32[2,2,64]{2,1,0:T(2,128)S(1)}, u32[]{:S(2)}, u32[]{:S(2)}) collective-permute-start(f32[2,2,64]{2,1,0:T(2,128)S(1)} %add_add_fusion.3), channel_id=1, source_target_pairs={{0,2},{2,4},{4,6},{6,8},{8,10},{10,12},{12,14},{1,3},{3,5},{5,7},{... | collective-permute-start | bytes 3080 | tf_op jit(solution)/shard_map/while/body/eval_jaxpr/ppermute | solution.py:35
  42.7 2.3 %collective-permute-start = (f32[2,1,64]{2,1,0:T(1,128)S(1)}, f32[2,1,64]{2,1,0:T(1,128)S(1)}, u32[]{:S(2)}, u32[]{:S(2)}) collective-permute-start(f32[2,1,64]{2,1,0:T(1,128)S(1)} %get-tuple-element.291), channel_id=1, source_target_pairs={{1,0},{0,1},{3,2},{2,3},{5,4},{4,5},{7,6},{6,7},{9,8},{8,9},{11,10... | collective-permute-start | bytes 1544 | tf_op jit(solution)/shard_map/while/body/eval_jaxpr/ppermute | solution.py:25
  45.6 1.1 collective-permute-start.2
  47.1 1.1 collective-permute-start.4
  48.8 1.1 collective-permute-start.6
  50.3 5.2 %collective-permute-start.8 = (f32[2,2,64]{2,1,0:T(2,128)S(1)}, f32[2,2,64]{2,1,0:T(2,128)S(1)}, u32[]{:S(2)}, u32[]{:S(2)}) collective-permute-start(f32[2,2,64]{2,1,0:T(2,128)S(1)} %add_add_fusion.3), channel_id=1, source_target_pairs={{0,2},{2,4},{4,6},{6,8},{8,10},{10,12},{12,14},{1,3},{3,5},{5,7},{... | collective-permute-start | bytes 3080 | tf_op jit(solution)/shard_map/while/body/eval_jaxpr/ppermute | solution.py:35
  55.5 2.3 %collective-permute-start = (f32[2,1,64]{2,1,0:T(1,128)S(1)}, f32[2,1,64]{2,1,0:T(1,128)S(1)}, u32[]{:S(2)}, u32[]{:S(2)}) collective-permute-start(f32[2,1,64]{2,1,0:T(1,128)S(1)} %get-tuple-element.291), channel_id=1, source_target_pairs={{1,0},{0,1},{3,2},{2,3},{5,4},{4,5},{7,6},{6,7},{9,8},{8,9},{11,10... | collective-permute-start | bytes 1544 | tf_op jit(solution)/shard_map/while/body/eval_jaxpr/ppermute | solution.py:25
  58.4 1.1 collective-permute-start.2
  60.0 1.1 collective-permute-start.4
  61.7 1.1 collective-permute-start.6
  63.1 5.2 %collective-permute-start.8 = (f32[2,2,64]{2,1,0:T(2,128)S(1)}, f32[2,2,64]{2,1,0:T(2,128)S(1)}, u32[]{:S(2)}, u32[]{:S(2)}) collective-permute-start(f32[2,2,64]{2,1,0:T(2,128)S(1)} %add_add_fusion.3), channel_id=1, source_target_pairs={{0,2},{2,4},{4,6},{6,8},{8,10},{10,12},{12,14},{1,3},{3,5},{5,7},{... | collective-permute-start | bytes 3080 | tf_op jit(solution)/shard_map/while/body/eval_jaxpr/ppermute | solution.py:35
  68.3 2.3 %collective-permute-start = (f32[2,1,64]{2,1,0:T(1,128)S(1)}, f32[2,1,64]{2,1,0:T(1,128)S(1)}, u32[]{:S(2)}, u32[]{:S(2)}) collective-permute-start(f32[2,1,64]{2,1,0:T(1,128)S(1)} %get-tuple-element.291), channel_id=1, source_target_pairs={{1,0},{0,1},{3,2},{2,3},{5,4},{4,5},{7,6},{6,7},{9,8},{8,9},{11,10... | collective-permute-start | bytes 1544 | tf_op jit(solution)/shard_map/while/body/eval_jaxpr/ppermute | solution.py:25
  71.2 1.1 collective-permute-start.2
  72.8 1.1 collective-permute-start.4
  74.5 1.1 collective-permute-start.6
  75.9 5.2 %collective-permute-start.8 = (f32[2,2,64]{2,1,0:T(2,128)S(1)}, f32[2,2,64]{2,1,0:T(2,128)S(1)}, u32[]{:S(2)}, u32[]{:S(2)}) collective-permute-start(f32[2,2,64]{2,1,0:T(2,128)S(1)} %add_add_fusion.3), channel_id=1, source_target_pairs={{0,2},{2,4},{4,6},{6,8},{8,10},{10,12},{12,14},{1,3},{3,5},{5,7},{... | collective-permute-start | bytes 3080 | tf_op jit(solution)/shard_map/while/body/eval_jaxpr/ppermute | solution.py:35
  81.2 2.3 %collective-permute-start = (f32[2,1,64]{2,1,0:T(1,128)S(1)}, f32[2,1,64]{2,1,0:T(1,128)S(1)}, u32[]{:S(2)}, u32[]{:S(2)}) collective-permute-start(f32[2,1,64]{2,1,0:T(1,128)S(1)} %get-tuple-element.291), channel_id=1, source_target_pairs={{1,0},{0,1},{3,2},{2,3},{5,4},{4,5},{7,6},{6,7},{9,8},{8,9},{11,10... | collective-permute-start | bytes 1544 | tf_op jit(solution)/shard_map/while/body/eval_jaxpr/ppermute | solution.py:25
  84.1 1.1 collective-permute-start.2
  85.6 1.1 collective-permute-start.4
  87.3 1.1 collective-permute-start.6
  88.8 5.2 %collective-permute-start.8 = (f32[2,2,64]{2,1,0:T(2,128)S(1)}, f32[2,2,64]{2,1,0:T(2,128)S(1)}, u32[]{:S(2)}, u32[]{:S(2)}) collective-permute-start(f32[2,2,64]{2,1,0:T(2,128)S(1)} %add_add_fusion.3), channel_id=1, source_target_pairs={{0,2},{2,4},{4,6},{6,8},{8,10},{10,12},{12,14},{1,3},{3,5},{5,7},{... | collective-permute-start | bytes 3080 | tf_op jit(solution)/shard_map/while/body/eval_jaxpr/ppermute | solution.py:35
  94.0 2.3 %collective-permute-start = (f32[2,1,64]{2,1,0:T(1,128)S(1)}, f32[2,1,64]{2,1,0:T(1,128)S(1)}, u32[]{:S(2)}, u32[]{:S(2)}) collective-permute-start(f32[2,1,64]{2,1,0:T(1,128)S(1)} %get-tuple-element.291), channel_id=1, source_target_pairs={{1,0},{0,1},{3,2},{2,3},{5,4},{4,5},{7,6},{6,7},{9,8},{8,9},{11,10... | collective-permute-start | bytes 1544 | tf_op jit(solution)/shard_map/while/body/eval_jaxpr/ppermute | solution.py:25
  96.9 1.1 collective-permute-start.2
  98.5 1.1 collective-permute-start.4
  100.2 1.1 collective-permute-start.6
  101.6 5.2 %collective-permute-start.8 = (f32[2,2,64]{2,1,0:T(2,128)S(1)}, f32[2,2,64]{2,1,0:T(2,128)S(1)}, u32[]{:S(2)}, u32[]{:S(2)}) collective-permute-start(f32[2,2,64]{2,1,0:T(2,128)S(1)} %add_add_fusion.3), channel_id=1, source_target_pairs={{0,2},{2,4},{4,6},{6,8},{8,10},{10,12},{12,14},{1,3},{3,5},{5,7},{... | collective-permute-start | bytes 3080 | tf_op jit(solution)/shard_map/while/body/eval_jaxpr/ppermute | solution.py:35
  106.8 2.3 %collective-permute-start = (f32[2,1,64]{2,1,0:T(1,128)S(1)}, f32[2,1,64]{2,1,0:T(1,128)S(1)}, u32[]{:S(2)}, u32[]{:S(2)}) collective-permute-start(f32[2,1,64]{2,1,0:T(1,128)S(1)} %get-tuple-element.291), channel_id=1, source_target_pairs={{1,0},{0,1},{3,2},{2,3},{5,4},{4,5},{7,6},{6,7},{9,8},{8,9},{11,10... | collective-permute-start | bytes 1544 | tf_op jit(solution)/shard_map/while/body/eval_jaxpr/ppermute | solution.py:25
  109.7 1.1 collective-permute-start.2
  111.3 1.1 collective-permute-start.4
  113.0 1.1 collective-permute-start.6
  114.4 5.2 %collective-permute-start.8 = (f32[2,2,64]{2,1,0:T(2,128)S(1)}, f32[2,2,64]{2,1,0:T(2,128)S(1)}, u32[]{:S(2)}, u32[]{:S(2)}) collective-permute-start(f32[2,2,64]{2,1,0:T(2,128)S(1)} %add_add_fusion.3), channel_id=1, source_target_pairs={{0,2},{2,4},{4,6},{6,8},{8,10},{10,12},{12,14},{1,3},{3,5},{5,7},{... | collective-permute-start | bytes 3080 | tf_op jit(solution)/shard_map/while/body/eval_jaxpr/ppermute | solution.py:35
  (32 other events, 36.2 us)
where the time goes:
time: 122 us; the launch traced here: 121 us
  waiting for transfers between devices  57.7 us (47%)
  starting transfers between devices  42.5 us (35%)
  local copies, waits for them, and re-layouts  12.3 us (10%)
  other arithmetic  5.93 us (5%)
  matrix products  1.72 us (1%)
    ppermute x8, waiting for transfers between devices, passed_along(): lax.ppermute(value, axis, [(source, source + steps) for source in range(i...  29.3 us
    ppermute x35, waiting for transfers between devices, with_halo(): lax.ppermute(head, axis, [((i + 1) % count, i) for i in range(count)])  19.9 us
    ppermute x35, starting transfers between devices, with_halo(): lax.ppermute(head, axis, [((i + 1) % count, i) for i in range(count)])  17.8 us
    ppermute x8, starting transfers between devices, passed_along(): lax.ppermute(value, axis, [(source, source + steps) for source in range(i...  16.8 us
    ppermute x35, waiting for transfers between devices, with_halo(): lax.ppermute(tail, axis, [(i, (i + 1) % count) for i in range(count)])  8.48 us
    ppermute x35, starting transfers between devices, with_halo(): lax.ppermute(tail, axis, [(i, (i + 1) % count) for i in range(count)])  7.86 us
    slice x70, local copies, waits for them, and re-layouts, burgers_rhs(): east = jnp.roll(center, -1, axis=-1)  5.72 us
  transfers between devices with their start and end apart: 78, of which 74 were waited for; matrix products, arithmetic and copies ran while one was open for 9% of the time, Pallas kernels for 0%

commit v1 on v0

v1 whole, which is shorter than its diff:
```python
import functools

import jax
import jax.numpy as jnp
import ml_dtypes
import numpy as np
from jax import lax
from jax.experimental import pallas as pl
from jax.experimental.pallas import tpu as pltpu
from jax.sharding import PartitionSpec as P

SWEEPS = 3
CSTEPS = 4
COARSEN = 4
SEGMENT_TIME = 0.5
VISCOSITY = 0.05
MESH = pl.DeviceIdType.MESH
CHUNKS = 4


def integration_table(count, length):
    last = count - 1
    orders = np.arange(count)
    angles = np.pi * (last - orders) / last
    points = np.cos(angles)
    cheb = np.cos(np.outer(angles, orders))
    weights = np.where((orders == 0) | (orders == last), 0.5, 1.0)
    inverse = 2.0 / last * weights[:, None] * cheb.T * weights[None, :]
    upper = orders + 1.0
    lower = np.maximum(orders - 1.0, 1.0)
    general = np.cos(np.outer(angles, upper)) / (2.0 * upper) - np.cos(
        np.outer(angles, orders - 1.0)
    ) / (2.0 * lower)
    general = general - (
        (-1.0) ** (orders + 1) / (2.0 * upper) - (-1.0) ** np.abs(orders - 1) / (2.0 * lower)
    )
    integral = np.where(
        orders[None, :] == 0,
        points[:, None] + 1.0,
        np.where(orders[None, :] == 1, (points[:, None] ** 2 - 1.0) / 2.0, general),
    )
    return (integral @ inverse * (length / 2.0)).astype(np.float32)


def split2(x):
    hi = x.astype(jnp.bfloat16)
    lo = (x - hi.astype(jnp.float32)).astype(jnp.bfloat16)
    return hi, lo


def tables(nodes, rows, cols):
    table = integration_table(nodes, SEGMENT_TIME)
    hi = table.astype(ml_dtypes.bfloat16)
    lo = (table - hi.astype(np.float32)).astype(ml_dtypes.bfloat16)
    eye = np.eye(rows, dtype=np.float32)
    big_hi = np.kron(hi.astype(np.float32), eye)
    big_lo = np.kron(lo.astype(np.float32), eye)
    big = np.concatenate([big_hi, big_hi, big_lo], axis=1).astype(ml_dtypes.bfloat16)
    coarse = cols // COARSEN
    fine_of = np.arange(cols)[:, None] // COARSEN
    copies = np.arange(2 * coarse)[None, :] % coarse
    down = (fine_of == copies).astype(np.float32) / (COARSEN * COARSEN)
    down = np.concatenate([down, down], axis=0).astype(ml_dtypes.bfloat16)
    up = (fine_of == copies).astype(np.float32).T.astype(ml_dtypes.bfloat16)
    return big, down, up


def coarse_prop(u, v):
    step_len = SEGMENT_TIME / CSTEPS
    spacing = float(COARSEN)
    a = step_len * VISCOSITY / (spacing * spacing)
    b = step_len / (2.0 * spacing)
    lanes = u.shape[1]
    for _ in range(CSTEPS):
        bu, bv = b * u, b * v
        cn, cs, ce, cw = a - bu, a + bu, a - bv, a + bv
        both = []
        for q in (u, v):
            north, south = pltpu.roll(q, 7, 0), pltpu.roll(q, 1, 0)
            east, west = pltpu.roll(q, lanes - 1, 1), pltpu.roll(q, 1, 1)
            both.append(
                ((1.0 - 4.0 * a) * q + (north * cn + south * cs)) + (east * ce + west * cw)
            )
        u, v = both
    return u, v


def row_sums(y):
    y = y + pltpu.roll(y, 1, 0)
    return y + pltpu.roll(y, 2, 0)


def kernel(
    nseg, x_hbm, t_hbm, r_hbm, p_hbm, swept_hbm, shift_ref,
    X, Sb, T, Rm, Pm, coarse0, jumps, prev, jsend, csend, ends,
    lsem, csem, xs_sem, xr_sem, js_sem, jr_sem, cs_sem, cr_sem, ps_sem, pr_sem, osem,
):
    seg = lax.axis_index("seg")
    space = lax.axis_index("space")
    other = 1 - space
    nodes, cols = X.shape[1], X.shape[4]
    rows = X.shape[3]
    per = nodes // CHUNKS
    depth = nodes * rows
    half = Rm.shape[1] // 2

    loads = []
    for c in range(CHUNKS):
        part = pl.ds(c * per, per)
        loads.append(pltpu.make_async_copy(x_hbm.at[0, part], X.at[0, part], lsem.at[c]))
        loads[-1].start()
    consts = [
        pltpu.make_async_copy(r_hbm, Rm, csem.at[0]),
        pltpu.make_async_copy(t_hbm, T, csem.at[1]),
        pltpu.make_async_copy(p_hbm, Pm, csem.at[2]),
    ]
    for copy in consts:
        copy.start()

    barrier = pltpu.get_barrier_semaphore()
    pl.semaphore_signal(
        barrier, inc=1, device_id={"space": other}, device_id_type=MESH
    )

    def greet(t, _):
        for s in range(2):
            pl.semaphore_signal(
                barrier, inc=1, device_id={"seg": t, "space": s}, device_id_type=MESH
            )
        return 0

    lax.fori_loop(0, seg, greet, 0)
    pl.semaphore_wait(barrier, 2 * (nseg - 1 - seg) + 1)

    swaps = []
    for c in range(CHUNKS):
        part = pl.ds(c * per, per)
        swaps.append(
            pltpu.make_async_remote_copy(
                src_ref=x_hbm.at[0, part], dst_ref=X.at[1, part],
                send_sem=xs_sem.at[c], recv_sem=xr_sem.at[c],
                device_id={"space": other}, device_id_type=MESH,
            )
        )
        swaps[-1].start()

    row_id = lax.broadcasted_iota(jnp.int32, (rows, cols), 0)
    top, bottom = row_id == rows - 1, row_id == 0
    lane_id = lax.broadcasted_iota(jnp.int32, (8, 2 * half), 1)
    left = lane_id < half

    def slope_pair(q_own, q_oth):
        up_own, up_oth = pltpu.roll(q_own, rows - 1, 0), pltpu.roll(q_oth, rows - 1, 0)
        dn_own, dn_oth = pltpu.roll(q_own, 1, 0), pltpu.roll(q_oth, 1, 0)
        return (
            (jnp.where(top, up_oth, up_own), jnp.where(bottom, dn_oth, dn_own)),
            (jnp.where(top, up_own, up_oth), jnp.where(bottom, dn_own, dn_oth)),
        )

    def node_slopes(m, strips):
        fields = [[X[s, m, c] for c in range(2)] for s in range(2)]
        vert = [slope_pair(fields[0][c], fields[1][c]) for c in range(2)]
        out = []
        for s in range(strips):
            hu, hv = 0.5 * fields[s][0], 0.5 * fields[s][1]
            cn, cs, ce, cw = VISCOSITY - hu, VISCOSITY + hu, VISCOSITY - hv, VISCOSITY + hv
            for c in range(2):
                q = fields[s][c]
                north, south = vert[c][s]
                east, west = pltpu.roll(q, cols - 1, 1), pltpu.roll(q, 1, 1)
                out.append(
                    (north * cn + south * cs)
                    + (east * ce + west * cw)
                    - (4.0 * VISCOSITY) * q
                )
        return out

    def slopes(first, count, strips):
        def body(j, _):
            m = 2 * j
            one, two = node_slopes(m, strips), node_slopes(m + 1, strips)
            for b in range(2 * strips):
                both = jnp.concatenate([one[b], two[b]], axis=0)
                hi, lo = split2(both)
                at = pl.multiple_of(j * (2 * rows), 2 * rows)
                lanes = pl.ds(b * cols, cols)
                Sb[pl.ds(at, 2 * rows), lanes] = hi
                Sb[pl.ds(depth + at, 2 * rows), lanes] = lo
                Sb[pl.ds(2 * depth + at, 2 * rows), lanes] = hi
            return 0

        lax.fori_loop(first // 2, (first + count) // 2, body, 0)

    def integrate(strips):
        for b in range(2 * strips):
            s, c = divmod(b, 2)
            total = jnp.dot(
                T[...], Sb[:, b * cols : (b + 1) * cols], preferred_element_type=jnp.float32
            )
            X[s, :, c] = X[s, 0, c][None] + total.reshape(nodes, rows, cols)

    def restrict_lanes(stack):
        hi, lo = split2(stack)
        return jnp.dot(
            jnp.concatenate([hi, lo], axis=1), Rm[...], preferred_element_type=jnp.float32
        )

    for c in range(CHUNKS):
        loads[c].wait()
        swaps[c].wait_recv()
        slopes(c * per, per, 2)

    consts[0].wait()
    starts = restrict_lanes(
        jnp.concatenate([X[0, 0, 0], X[0, 0, 1], X[1, 0, 0], X[1, 0, 1]], axis=0)
    )
    sums = [row_sums(starts[8 * b : 8 * b + 8]) for b in range(4)]

    def ends_of(y):
        return [y[3:4], y[7:8]]

    su = jnp.concatenate((ends_of(sums[0]) + ends_of(sums[2])) * 2, axis=0)
    sv = jnp.concatenate((ends_of(sums[1]) + ends_of(sums[3])) * 2, axis=0)
    packed = jnp.where(left, su, sv)
    csend[...] = packed[0:4]

    def coarse_copy(t):
        return pltpu.make_async_remote_copy(
            src_ref=csend, dst_ref=coarse0, send_sem=cs_sem.at[t], recv_sem=cr_sem,
            device_id={"seg": t}, device_id_type=MESH,
        )

    @pl.when(seg == 0)
    def _():
        for t in range(nseg - 1, 0, -1):
            coarse_copy(t).start()

    gu, gv = coarse_prop(su, sv)
    gpack = jnp.where(left, gu, gv)

    consts[1].wait()
    integrate(2)
    slopes(0, nodes, 2)
    integrate(2)
    slopes(0, nodes, 1)

    tail = jnp.dot(
        T[depth - 2 * rows :, :], Sb[:, : 2 * cols], preferred_element_type=jnp.float32
    )[rows:]
    eu = X[0, 0, 0] + tail[:, :cols]
    ev = X[0, 0, 1] + tail[:, cols:]
    ends[0] = eu
    ends[1] = ev
    finish = restrict_lanes(jnp.concatenate([eu, ev], axis=0))
    fpack = row_sums(jnp.where(left, finish[:8], finish[8:]))
    jsend[0:1] = fpack[3:4] - gpack[0:1]
    jsend[1:2] = fpack[7:8] - gpack[1:2]

    def jump_copy(t, s, way):
        return pltpu.make_async_remote_copy(
            src_ref=jsend, dst_ref=jumps.at[seg, way],
            send_sem=js_sem.at[t, way], recv_sem=jr_sem.at[seg, way],
            device_id={"seg": t, "space": s}, device_id_type=MESH,
        )

    def send_jump(i, _):
        t = nseg - 1 - i
        jump_copy(t, space, 0).start()
        jump_copy(t, other, 1).start()
        return 0

    lax.fori_loop(0, nseg - 1 - seg, send_jump, 0)

    end_copy = pltpu.make_async_remote_copy(
        src_ref=ends, dst_ref=prev, send_sem=ps_sem, recv_sem=pr_sem,
        device_id={"seg": lax.rem(seg + 1, nseg)}, device_id_type=MESH,
    )

    @pl.when(seg < nseg - 1)
    def _():
        end_copy.start()

    integrate(1)
    store = pltpu.make_async_copy(X.at[0], swept_hbm, osem)
    store.start()
    consts[2].wait()

    def expand(x):
        y = pltpu.roll(x, half, 1)
        return jnp.where(left, x, y), jnp.where(left, y, x)

    @pl.when(seg == 0)
    def _():
        shift_ref[...] = jnp.zeros_like(shift_ref)

    @pl.when(seg > 0)
    def _():
        coarse_copy(0).wait_recv()
        c = coarse0[...]
        u, v = expand(jnp.concatenate([c, c], axis=0))

        def advance(i, carry):
            u, v = coarse_prop(*carry)
            for way in range(2):
                pltpu.make_async_copy(jsend, jumps.at[i, way], jr_sem.at[i, way]).wait()
            own, oth = jumps[i, 0], jumps[i, 1]
            du, dv = expand(jnp.concatenate([own, oth, own, oth], axis=0))
            return u + du, v + dv

        u, v = lax.fori_loop(0, seg, advance, (u, v))
        end_copy.wait_recv()
        pu, pv = prev[0], prev[1]
        back = restrict_lanes(jnp.concatenate([pu, pv], axis=0))
        lower = lax.broadcasted_iota(jnp.int32, (8, 2 * half), 0) < 4
        spread = []
        for q, r in ((u, row_sums(back[:8])), (v, row_sums(back[8:]))):
            d0 = jnp.broadcast_to(q[0:1] - r[3:4], (8, 2 * half))
            d1 = jnp.broadcast_to(q[1:2] - r[7:8], (8, 2 * half))
            hi, lo = split2(jnp.where(lower, d0, d1))
            spread.append(
                jnp.where(left, hi.astype(jnp.float32), lo.astype(jnp.float32))
            )
        wide = jnp.dot(
            jnp.concatenate(spread, axis=0).astype(jnp.bfloat16), Pm[...],
            preferred_element_type=jnp.float32,
        )
        shift_ref[0] = (pu + wide[:8]) - X[0, 0, 0]
        shift_ref[1] = (pv + wide[8:]) - X[0, 0, 1]

    for copy in swaps:
        copy.wait_send()

    @pl.when(seg == 0)
    def _():
        for t in range(nseg - 1, 0, -1):
            coarse_copy(t).wait_send()

    def sent(i, _):
        t = nseg - 1 - i
        jump_copy(t, space, 0).wait_send()
        jump_copy(t, other, 1).wait_send()
        return 0

    lax.fori_loop(0, nseg - 1 - seg, sent, 0)

    @pl.when(seg < nseg - 1)
    def _():
        end_copy.wait_send()

    store.wait()


def per_device(nseg, trajectory):
    _, nodes, comps, rows, cols = trajectory.shape
    big, down, up = tables(nodes, rows, cols)
    depth = nodes * rows
    half = cols // COARSEN
    crows = rows // COARSEN
    bf16, f32 = jnp.bfloat16, jnp.float32
    DMA = pltpu.SemaphoreType.DMA
    anywhere = pl.BlockSpec(memory_space=pl.ANY)
    swept, shift = pl.pallas_call(
        functools.partial(kernel, nseg),
        out_shape=(
            jax.ShapeDtypeStruct((nodes, comps, rows, cols), f32),
            jax.ShapeDtypeStruct((comps, rows, cols), f32),
        ),
        in_specs=[anywhere] * 4,
        out_specs=(anywhere, pl.BlockSpec(memory_space=pltpu.VMEM)),
        scratch_shapes=[
            pltpu.VMEM((2, nodes, comps, rows, cols), f32),
            pltpu.VMEM((3 * depth, 2 * comps * cols), bf16),
            pltpu.VMEM(big.shape, bf16),
            pltpu.VMEM(down.shape, bf16),
            pltpu.VMEM(up.shape, bf16),
            pltpu.VMEM((2 * crows, 2 * half), f32),
            pltpu.VMEM((nseg, 2, crows, 2 * half), f32),
            pltpu.VMEM((comps, rows, cols), f32),
            pltpu.VMEM((crows, 2 * half), f32),
            pltpu.VMEM((2 * crows, 2 * half), f32),
            pltpu.VMEM((comps, rows, cols), f32),
            DMA((CHUNKS,)), DMA((3,)), DMA((CHUNKS,)), DMA((CHUNKS,)),
            DMA((nseg, 2)), DMA((nseg, 2)), DMA((nseg,)), DMA, DMA, DMA, DMA,
        ],
        compiler_params=pltpu.CompilerParams(
            collective_id=0, has_side_effects=True, vmem_limit_bytes=24 * 2**20
        ),
    )(trajectory, jnp.asarray(big), jnp.asarray(down), jnp.asarray(up))
    return (swept + shift[None])[None]


def solution(mesh):
    spec = P(("groups", "seg"), None, None, "space", None)
    return jax.shard_map(
        functools.partial(per_device, mesh.shape["seg"]),
        mesh=mesh,
        in_specs=(spec,),
        out_specs=spec,
        check_vma=False,
    )
```

time: 122 us -> 23.5 us (0.19)
  the two profiles are of different devices: /device:TPU:27 before, /device:TPU:31 now
where the time goes in v1:
time: 23.5 us; the launch traced here: 23.2 us
  Pallas kernels  18.6 us (79%)
  local copies, waits for them, and re-layouts  3.78 us (16%)
  other arithmetic  0.83 us (4%)
    pallas_call x1, Pallas kernels, per_device(): pl.pallas_call(functools.partial(kernel, nseg), out_shape=(jax.ShapeDtype...  18.6 us
    unnamed x8, local copies, waits for them, and re-layouts  3.78 us
    broadcast_in_dim x1, other arithmetic, per_device(): return (swept + shift[None])[None]  0.83 us

profile of v1, /device:TPU:31, one launch (start us, length us, event | category | flops | bytes accessed | tf_op | source)
XLA Modules:
  0.0 23.2 jit_solution(4905789797700782501)
XLA Ops:
  0.0 0.0 copy-start
  0.0 1.0 %copy-done = f32[1,32,2,8,256]{4,3,2,1,0:T(8,128)S(1)} copy-done((f32[1,32,2,8,256]{4,3,2,1,0:T(8,128)S(1)}, f32[1,32,2,8,256]{4,3,2,1,0:T(8,128)}, u32[]{:S(2)}) %copy-start) | copy-done | bytes 524312
  1.0 0.0 copy-start.1
  1.0 1.0 %copy-done.1 = bf16[256,768]{1,0:T(8,128)(2,1)S(1)} copy-done((bf16[256,768]{1,0:T(8,128)(2,1)S(1)}, bf16[256,768]{1,0:T(8,128)(2,1)}, u32[]{:S(2)}) %copy-start.1) | copy-done | bytes 393240
  2.0 0.0 copy-start.2
  2.0 0.9 %copy-done.2 = bf16[512,128]{1,0:T(8,128)(2,1)S(1)} copy-done((bf16[512,128]{1,0:T(8,128)(2,1)S(1)}, bf16[512,128]{1,0:T(8,128)(2,1)}, u32[]{:S(2)}) %copy-start.2) | copy-done | bytes 131096
  2.9 0.0 copy-start.3
  2.9 0.8 %copy-done.3 = bf16[128,256]{1,0:T(8,128)(2,1)S(1)} copy-done((bf16[128,256]{1,0:T(8,128)(2,1)S(1)}, bf16[128,256]{1,0:T(8,128)(2,1)}, u32[]{:S(2)}) %copy-start.3) | copy-done | bytes 65560
  3.8 18.6 %shard_map.46 = (f32[32,2,8,256]{3,2,1,0:T(8,128)S(1)}, f32[2,8,256]{2,1,0:T(8,128)S(1)}) custom-call(f32[1,32,2,8,256]{4,3,2,1,0:T(8,128)S(1)} %copy-done, bf16[256,768]{1,0:T(8,128)(2,1)S(1)} %copy-done.1, bf16[512,128]{1,0:T(8,128)(2,1)S(1)} %copy-done.2, bf16[128,256]{1,0:T(8,128)(2,1)S(1)} %copy-done.3), custom_call_target="tpu_custom_call" | custom-call | tf_op jit(solution)/shard_map/pallas_call | solution.py:362
  22.4 0.8 %add_bitcast_fusion = f32[1,32,2,8,256]{4,3,2,1,0:T(8,128)} fusion(f32[32,2,8,256]{3,2,1,0:T(8,128)S(1)} %get-tuple-element.7, f32[2,8,256]{2,1,0:T(8,128)S(1)} %get-tuple-element.8), kind=kLoop, calls=%fused_computation | loop fusion | flops 131072 | bytes 1064960 | tf_op jit(solution)/shard_map/broadcast_in_dim | solution.py:389
Async XLA Ops:
  0.0 1.0 %copy-start = (f32[1,32,2,8,256]{4,3,2,1,0:T(8,128)S(1)}, f32[1,32,2,8,256]{4,3,2,1,0:T(8,128)}, u32[]{:S(2)}) copy-start(f32[1,32,2,8,256]{4,3,2,1,0:T(8,128)} %x_hbm.1) | copy-start | bytes 1572868
  1.0 1.0 %copy-start.1 = (bf16[256,768]{1,0:T(8,128)(2,1)S(1)}, bf16[256,768]{1,0:T(8,128)(2,1)}, u32[]{:S(2)}) copy-start(bf16[256,768]{1,0:T(8,128)(2,1)} %constant.6.clone.t_hbm) | copy-start | bytes 1179652
  2.0 0.9 %copy-start.2 = (bf16[512,128]{1,0:T(8,128)(2,1)S(1)}, bf16[512,128]{1,0:T(8,128)(2,1)}, u32[]{:S(2)}) copy-start(bf16[512,128]{1,0:T(8,128)(2,1)} %constant.7.clone.r_hbm) | copy-start | bytes 393220
  2.9 0.8 %copy-start.3 = (bf16[128,256]{1,0:T(8,128)(2,1)S(1)}, bf16[128,256]{1,0:T(8,128)(2,1)}, u32[]{:S(2)}) copy-start(bf16[128,256]{1,0:T(8,128)(2,1)} %constant.8.clone.p_hbm) | copy-start | bytes 196612

commit v2 on v1

--- a/solution.py
+++ b/solution.py
@@ -94,6 +94,7 @@
     nseg, x_hbm, t_hbm, r_hbm, p_hbm, swept_hbm, shift_ref,
     X, Sb, T, Rm, Pm, coarse0, jumps, prev, jsend, csend, ends,
     lsem, csem, xs_sem, xr_sem, js_sem, jr_sem, cs_sem, cr_sem, ps_sem, pr_sem, osem,
+    hello, ready,
 ):
     seg = lax.axis_index("seg")
     space = lax.axis_index("space")
@@ -118,19 +119,31 @@
         copy.start()
 
     barrier = pltpu.get_barrier_semaphore()
-    pl.semaphore_signal(
-        barrier, inc=1, device_id={"space": other}, device_id_type=MESH
-    )
+
+    @pl.when(space == 0)
+    def _():
+        pl.semaphore_signal(
+            barrier, inc=1, device_id={"space": 1}, device_id_type=MESH
+        )
 
     def greet(t, _):
-        for s in range(2):
-            pl.semaphore_signal(
-                barrier, inc=1, device_id={"seg": t, "space": s}, device_id_type=MESH
-            )
+        pl.semaphore_signal(
+            barrier, inc=1, device_id={"seg": t, "space": 0}, device_id_type=MESH
+        )
         return 0
 
     lax.fori_loop(0, seg, greet, 0)
-    pl.semaphore_wait(barrier, 2 * (nseg - 1 - seg) + 1)
+
+    @pl.when(space == 1)
+    def _():
+        pl.semaphore_wait(barrier, 1)
+        pl.semaphore_signal(
+            hello, inc=1, device_id={"space": 0}, device_id_type=MESH
+        )
+
+    @pl.when(space == 0)
+    def _():
+        pl.semaphore_wait(hello, 1)
 
     swaps = []
     for c in range(CHUNKS):
@@ -189,7 +202,7 @@
                 Sb[pl.ds(2 * depth + at, 2 * rows), lanes] = hi
             return 0
 
-        lax.fori_loop(first // 2, (first + count) // 2, body, 0)
+        lax.fori_loop(first // 2, (first + count) // 2, body, 0, unroll=4)
 
     def integrate(strips):
         for b in range(2 * strips):
@@ -230,11 +243,6 @@
             device_id={"seg": t}, device_id_type=MESH,
         )
 
-    @pl.when(seg == 0)
-    def _():
-        for t in range(nseg - 1, 0, -1):
-            coarse_copy(t).start()
-
     gu, gv = coarse_prop(su, sv)
     gpack = jnp.where(left, gu, gv)
 
@@ -243,6 +251,24 @@
     slopes(0, nodes, 2)
     integrate(2)
     slopes(0, nodes, 1)
+
+    @pl.when(seg < nseg - 1)
+    def _():
+        @pl.when(space == 0)
+        def _():
+            pl.semaphore_wait(barrier, 2 * (nseg - 1 - seg))
+            pl.semaphore_signal(
+                ready, inc=1, device_id={"space": 1}, device_id_type=MESH
+            )
+
+        @pl.when(space == 1)
+        def _():
+            pl.semaphore_wait(ready, 1)
+
+    @pl.when(seg == 0)
+    def _():
+        for t in range(nseg - 1, 0, -1):
+            coarse_copy(t).start()
 
     tail = jnp.dot(
         T[depth - 2 * rows :, :], Sb[:, : 2 * cols], preferred_element_type=jnp.float32
@@ -381,9 +407,10 @@
             pltpu.VMEM((comps, rows, cols), f32),
             DMA((CHUNKS,)), DMA((3,)), DMA((CHUNKS,)), DMA((CHUNKS,)),
             DMA((nseg, 2)), DMA((nseg, 2)), DMA((nseg,)), DMA, DMA, DMA, DMA,
+            pltpu.SemaphoreType.REGULAR, pltpu.SemaphoreType.REGULAR,
         ],
         compiler_params=pltpu.CompilerParams(
-            collective_id=0, has_side_effects=True, vmem_limit_bytes=24 * 2**20
+            collective_id=0, has_side_effects=True, vmem_limit_bytes=60 * 2**20
         ),
     )(trajectory, jnp.asarray(big), jnp.asarray(down), jnp.asarray(up))
     return (swept + shift[None])[None]

time: 23.5 us -> 14 us (0.60)
  the two profiles are of different devices: /device:TPU:31 before, /device:TPU:27 now
where the time goes in v2:
time: 14 us; the launch traced here: 13.9 us
  Pallas kernels  12 us (86%)
  other arithmetic  1.88 us (13%)
    pallas_call x1, Pallas kernels, per_device(): pl.pallas_call(functools.partial(kernel, nseg), out_shape=(jax.ShapeDtype...  12 us
    broadcast_in_dim x1, other arithmetic, per_device(): return (swept + shift[None])[None]  1.88 us

profile of v2, /device:TPU:27, one launch (start us, length us, event | category | flops | bytes accessed | tf_op | source)
XLA Modules:
  0.0 13.9 jit_solution(14044989693858548912)
XLA Ops:
  0.0 12.0 %shard_map.46 = (f32[32,2,8,256]{3,2,1,0:T(8,128)}, f32[2,8,256]{2,1,0:T(8,128)}) custom-call(f32[1,32,2,8,256]{4,3,2,1,0:T(8,128)} %x_hbm.1, bf16[256,768]{1,0:T(8,128)(2,1)} %constant.6.clone.t_hbm, bf16[512,128]{1,0:T(8,128)(2,1)} %constant.7.clone.r_hbm, bf16[128,256]{1,0:T(8,128)(2,1)} %constant.8.clone.p_hbm), custom_call_target="tpu_custom_call" | custom-call | tf_op jit(solution)/shard_map/pallas_call | solution.py:388
  12.0 1.9 %add_bitcast_fusion = f32[1,32,2,8,256]{4,3,2,1,0:T(8,128)} fusion(f32[32,2,8,256]{3,2,1,0:T(8,128)} %get-tuple-element.7, f32[2,8,256]{2,1,0:T(8,128)} %get-tuple-element.8), kind=kLoop, calls=%fused_computation | loop fusion | flops 131072 | bytes 1064960 | tf_op jit(solution)/shard_map/broadcast_in_dim | solution.py:416

commit v3 on v2

--- a/solution.py
+++ b/solution.py
@@ -91,7 +91,7 @@
 
 
 def kernel(
-    nseg, x_hbm, t_hbm, r_hbm, p_hbm, swept_hbm, shift_ref,
+    nseg, x_hbm, t_hbm, swept_hbm, shift_ref,
     X, Sb, T, Rm, Pm, coarse0, jumps, prev, jsend, csend, ends,
     lsem, csem, xs_sem, xr_sem, js_sem, jr_sem, cs_sem, cr_sem, ps_sem, pr_sem, osem,
     hello, ready,
@@ -110,10 +110,19 @@
         part = pl.ds(c * per, per)
         loads.append(pltpu.make_async_copy(x_hbm.at[0, part], X.at[0, part], lsem.at[c]))
         loads[-1].start()
+    wide, narrow = T.shape[1], Rm.shape[1]
+    below = pl.ds(0, Pm.shape[0])
     consts = [
-        pltpu.make_async_copy(r_hbm, Rm, csem.at[0]),
-        pltpu.make_async_copy(t_hbm, T, csem.at[1]),
-        pltpu.make_async_copy(p_hbm, Pm, csem.at[2]),
+        pltpu.make_async_copy(
+            t_hbm.at[:, pl.ds(wide, narrow)], Rm.at[pl.ds(0, cols)], csem.at[0]
+        ),
+        pltpu.make_async_copy(
+            t_hbm.at[:, pl.ds(wide + narrow, narrow)], Rm.at[pl.ds(cols, cols)], csem.at[1]
+        ),
+        pltpu.make_async_copy(t_hbm.at[:, pl.ds(0, wide)], T, csem.at[2]),
+        pltpu.make_async_copy(
+            t_hbm.at[below, pl.ds(wide + 2 * narrow, cols)], Pm, csem.at[3]
+        ),
     ]
     for copy in consts:
         copy.start()
@@ -202,7 +211,7 @@
                 Sb[pl.ds(2 * depth + at, 2 * rows), lanes] = hi
             return 0
 
-        lax.fori_loop(first // 2, (first + count) // 2, body, 0, unroll=4)
+        lax.fori_loop(first // 2, (first + count) // 2, body, 0, unroll=True)
 
     def integrate(strips):
         for b in range(2 * strips):
@@ -224,6 +233,7 @@
         slopes(c * per, per, 2)
 
     consts[0].wait()
+    consts[1].wait()
     starts = restrict_lanes(
         jnp.concatenate([X[0, 0, 0], X[0, 0, 1], X[1, 0, 0], X[1, 0, 1]], axis=0)
     )
@@ -246,7 +256,7 @@
     gu, gv = coarse_prop(su, sv)
     gpack = jnp.where(left, gu, gv)
 
-    consts[1].wait()
+    consts[2].wait()
     integrate(2)
     slopes(0, nodes, 2)
     integrate(2)
@@ -309,7 +319,7 @@
     integrate(1)
     store = pltpu.make_async_copy(X.at[0], swept_hbm, osem)
     store.start()
-    consts[2].wait()
+    consts[3].wait()
 
     def expand(x):
         y = pltpu.roll(x, half, 1)
@@ -381,6 +391,11 @@
     big, down, up = tables(nodes, rows, cols)
     depth = nodes * rows
     half = cols // COARSEN
+    table = np.zeros((depth, 3 * depth + 4 * half + cols), big.dtype)
+    table[:, : 3 * depth] = big
+    table[:, 3 * depth : 3 * depth + 2 * half] = down[:cols]
+    table[:, 3 * depth + 2 * half : 3 * depth + 4 * half] = down[cols:]
+    table[: 2 * half, 3 * depth + 4 * half :] = up
     crows = rows // COARSEN
     bf16, f32 = jnp.bfloat16, jnp.float32
     DMA = pltpu.SemaphoreType.DMA
@@ -391,7 +406,7 @@
             jax.ShapeDtypeStruct((nodes, comps, rows, cols), f32),
             jax.ShapeDtypeStruct((comps, rows, cols), f32),
         ),
-        in_specs=[anywhere] * 4,
+        in_specs=[anywhere] * 2,
         out_specs=(anywhere, pl.BlockSpec(memory_space=pltpu.VMEM)),
         scratch_shapes=[
             pltpu.VMEM((2, nodes, comps, rows, cols), f32),
@@ -405,14 +420,14 @@
             pltpu.VMEM((crows, 2 * half), f32),
             pltpu.VMEM((2 * crows, 2 * half), f32),
             pltpu.VMEM((comps, rows, cols), f32),
-            DMA((CHUNKS,)), DMA((3,)), DMA((CHUNKS,)), DMA((CHUNKS,)),
+            DMA((CHUNKS,)), DMA((4,)), DMA((CHUNKS,)), DMA((CHUNKS,)),
             DMA((nseg, 2)), DMA((nseg, 2)), DMA((nseg,)), DMA, DMA, DMA, DMA,
             pltpu.SemaphoreType.REGULAR, pltpu.SemaphoreType.REGULAR,
         ],
         compiler_params=pltpu.CompilerParams(
-            collective_id=0, has_side_effects=True, vmem_limit_bytes=60 * 2**20
+            collective_id=0, has_side_effects=True, vmem_limit_bytes=54400 * 1024
         ),
-    )(trajectory, jnp.asarray(big), jnp.asarray(down), jnp.asarray(up))
+    )(trajectory, jnp.asarray(table))
     return (swept + shift[None])[None]
 
 

time: 14 us -> 11.7 us (0.84)
  Pallas kernels: 12 us -> 10.7 us
  other arithmetic: 1.88 us -> 0.83 us
    pallas_call x1, Pallas kernels: 12 us -> 10.7 us  [per_device(): pl.pallas_call(functools.partial(kernel, nseg), out_shape=(jax.ShapeDtype...]
    broadcast_in_dim x1, other arithmetic: 1.88 us -> 0.83 us  [per_device(): return (swept + shift[None])[None]]
where the time goes in v3:
time: 11.7 us; the launch traced here: 11.6 us
  Pallas kernels  10.7 us (91%)
  other arithmetic  0.83 us (7%)
    pallas_call x1, Pallas kernels, per_device(): pl.pallas_call(functools.partial(kernel, nseg), out_shape=(jax.ShapeDtype...  10.7 us
    broadcast_in_dim x1, other arithmetic, per_device(): return (swept + shift[None])[None]  0.83 us

profile of v3, /device:TPU:27, one launch (start us, length us, event | category | flops | bytes accessed | tf_op | source)
XLA Modules:
  0.0 11.6 jit_solution(15163655751572503686)
XLA Ops:
  0.0 10.7 %shard_map.28 = (f32[32,2,8,256]{3,2,1,0:T(8,128)S(1)}, f32[2,8,256]{2,1,0:T(8,128)S(1)}) custom-call(f32[1,32,2,8,256]{4,3,2,1,0:T(8,128)} %x_hbm.1, bf16[256,1280]{1,0:T(8,128)(2,1)} %constant.2.clone.t_hbm), custom_call_target="tpu_custom_call" | custom-call | tf_op jit(solution)/shard_map/pallas_call | solution.py:403
  10.7 0.8 %add_bitcast_fusion = f32[1,32,2,8,256]{4,3,2,1,0:T(8,128)} fusion(f32[32,2,8,256]{3,2,1,0:T(8,128)S(1)} %get-tuple-element.7, f32[2,8,256]{2,1,0:T(8,128)S(1)} %get-tuple-element.8), kind=kLoop, calls=%fused_computation | loop fusion | flops 131072 | bytes 1064960 | tf_op jit(solution)/shard_map/broadcast_in_dim | solution.py:431

commit v4 on v3

--- a/solution.py
+++ b/solution.py
@@ -208,7 +208,6 @@
                 lanes = pl.ds(b * cols, cols)
                 Sb[pl.ds(at, 2 * rows), lanes] = hi
                 Sb[pl.ds(depth + at, 2 * rows), lanes] = lo
-                Sb[pl.ds(2 * depth + at, 2 * rows), lanes] = hi
             return 0
 
         lax.fori_loop(first // 2, (first + count) // 2, body, 0, unroll=True)
@@ -216,8 +215,11 @@
     def integrate(strips):
         for b in range(2 * strips):
             s, c = divmod(b, 2)
+            lanes = slice(b * cols, (b + 1) * cols)
             total = jnp.dot(
-                T[...], Sb[:, b * cols : (b + 1) * cols], preferred_element_type=jnp.float32
+                T[:, : 2 * depth], Sb[:, lanes], preferred_element_type=jnp.float32
+            ) + jnp.dot(
+                T[:, 2 * depth :], Sb[:depth, lanes], preferred_element_type=jnp.float32
             )
             X[s, :, c] = X[s, 0, c][None] + total.reshape(nodes, rows, cols)
 
@@ -280,8 +282,15 @@
         for t in range(nseg - 1, 0, -1):
             coarse_copy(t).start()
 
-    tail = jnp.dot(
-        T[depth - 2 * rows :, :], Sb[:, : 2 * cols], preferred_element_type=jnp.float32
+    tail = (
+        jnp.dot(
+            T[depth - 2 * rows :, : 2 * depth], Sb[:, : 2 * cols],
+            preferred_element_type=jnp.float32,
+        )
+        + jnp.dot(
+            T[depth - 2 * rows :, 2 * depth :], Sb[:depth, : 2 * cols],
+            preferred_element_type=jnp.float32,
+        )
     )[rows:]
     eu = X[0, 0, 0] + tail[:, :cols]
     ev = X[0, 0, 1] + tail[:, cols:]
@@ -410,7 +419,7 @@
         out_specs=(anywhere, pl.BlockSpec(memory_space=pltpu.VMEM)),
         scratch_shapes=[
             pltpu.VMEM((2, nodes, comps, rows, cols), f32),
-            pltpu.VMEM((3 * depth, 2 * comps * cols), bf16),
+            pltpu.VMEM((2 * depth, 2 * comps * cols), bf16),
             pltpu.VMEM(big.shape, bf16),
             pltpu.VMEM(down.shape, bf16),
             pltpu.VMEM(up.shape, bf16),

time: 11.7 us -> 11.7 us (level)
  no operation moved by 1% of the time
where the time goes in v4:
time: 11.7 us; the launch traced here: 11.5 us
  Pallas kernels  10.7 us (91%)
  other arithmetic  0.83 us (7%)
    pallas_call x1, Pallas kernels, per_device(): pl.pallas_call(functools.partial(kernel, nseg), out_shape=(jax.ShapeDtype...  10.7 us
    broadcast_in_dim x1, other arithmetic, per_device(): return (swept + shift[None])[None]  0.83 us

profile of v4, /device:TPU:27, one launch (start us, length us, event | category | flops | bytes accessed | tf_op | source)
XLA Modules:
  0.0 11.5 jit_solution(7431358088664481248)
XLA Ops:
  0.0 10.7 %shard_map.28 = (f32[32,2,8,256]{3,2,1,0:T(8,128)S(1)}, f32[2,8,256]{2,1,0:T(8,128)S(1)}) custom-call(f32[1,32,2,8,256]{4,3,2,1,0:T(8,128)} %x_hbm.1, bf16[256,1280]{1,0:T(8,128)(2,1)} %constant.2.clone.t_hbm), custom_call_target="tpu_custom_call" | custom-call | tf_op jit(solution)/shard_map/pallas_call | solution.py:412
  10.7 0.8 %add_bitcast_fusion = f32[1,32,2,8,256]{4,3,2,1,0:T(8,128)} fusion(f32[32,2,8,256]{3,2,1,0:T(8,128)S(1)} %get-tuple-element.7, f32[2,8,256]{2,1,0:T(8,128)S(1)} %get-tuple-element.8), kind=kLoop, calls=%fused_computation | loop fusion | flops 131072 | bytes 1064960 | tf_op jit(solution)/shard_map/broadcast_in_dim | solution.py:440

commit v5 on v4

--- a/solution.py
+++ b/solution.py
@@ -262,8 +262,6 @@
     integrate(2)
     slopes(0, nodes, 2)
     integrate(2)
-    slopes(0, nodes, 1)
-
     @pl.when(seg < nseg - 1)
     def _():
         @pl.when(space == 0)
@@ -281,6 +279,8 @@
     def _():
         for t in range(nseg - 1, 0, -1):
             coarse_copy(t).start()
+
+    slopes(0, nodes, 1)
 
     tail = (
         jnp.dot(

time: 11.7 us -> 11.8 us (level)
    pallas_call x1, Pallas kernels: 10.7 us -> 10.8 us  [per_device(): pl.pallas_call(functools.partial(kernel, nseg), out_shape=(jax.ShapeDtype...]
where the time goes in v5:
time: 11.8 us; the launch traced here: 11.7 us
  Pallas kernels  10.8 us (92%)
  other arithmetic  0.83 us (7%)
    pallas_call x1, Pallas kernels, per_device(): pl.pallas_call(functools.partial(kernel, nseg), out_shape=(jax.ShapeDtype...  10.8 us
    broadcast_in_dim x1, other arithmetic, per_device(): return (swept + shift[None])[None]  0.83 us

profile of v5, /device:TPU:27, one launch (start us, length us, event | category | flops | bytes accessed | tf_op | source)
XLA Modules:
  0.0 11.7 jit_solution(14685625637204712879)
XLA Ops:
  0.0 10.8 %shard_map.28 = (f32[32,2,8,256]{3,2,1,0:T(8,128)S(1)}, f32[2,8,256]{2,1,0:T(8,128)S(1)}) custom-call(f32[1,32,2,8,256]{4,3,2,1,0:T(8,128)} %x_hbm.1, bf16[256,1280]{1,0:T(8,128)(2,1)} %constant.2.clone.t_hbm), custom_call_target="tpu_custom_call" | custom-call | tf_op jit(solution)/shard_map/pallas_call | solution.py:412
  10.8 0.8 %add_bitcast_fusion = f32[1,32,2,8,256]{4,3,2,1,0:T(8,128)} fusion(f32[32,2,8,256]{3,2,1,0:T(8,128)S(1)} %get-tuple-element.7, f32[2,8,256]{2,1,0:T(8,128)S(1)} %get-tuple-element.8), kind=kLoop, calls=%fused_computation | loop fusion | flops 131072 | bytes 1064960 | tf_op jit(solution)/shard_map/broadcast_in_dim | solution.py:440
